TPU v7x, 128 devices: a whole 4x4x4 slice. The times are simulated.
128 devices in a mesh: dp: 16 (over x, y), vocab: 8 (over z, core).
Axes of the slice: x: 4, y: 4, z: 4, core: 2. Of those that a mesh axis runs over, the one named last changes fastest.
Arguments:
- pol_hidden: bfloat16 [512, 8192], P(None, 'dp'), may hold values from -82 to 82
- pol_weight: bfloat16 [8192, 65536], P('dp', 'vocab'), may hold values from -0.0625 to 0.0625
- ref_logits: bfloat16 [256, 65536], P('dp', 'vocab'), may hold values from -205 to 205
- targets: int32 [256], replicated, may hold values from 0 to 65535
- owners: int32 [256, 1], replicated, may hold values from 0 to 15; in each aligned block of 16 rows (0 to 15, 16 to 31, ...) at most 2 rows name the same one
- grad_logprob: float32 [512], replicated, may hold values from -9 to 9
- grad_kl: float32 [512], replicated, may hold values from -96 to 96
Outputs:
- token_logprob: float32 [512], P('dp')
- token_kl: float32 [512], P('dp')
- normalizer: float32 [512], P('dp')
- feature_grad: bfloat16 [512, 8192], P('vocab', 'dp')
- weight_grad: bfloat16 [8192, 65536], P('dp', 'vocab')
Inputs may be any that keep to these rules, and one draw needn't show every extreme that they name: `owners`: in each aligned block of 16 rows (the rows of one device along dp) no owner is named more than 2 times, a bound that some block reaches.
All inputs are finite; a program needn't handle non-finite values.
Results may differ from a plain program's by a relative error of at most 0.015.
Values may be sent and summed in bfloat16 or wider, within the bound.
A program may use at most 128 MiB of HBM per device.

v0:
```python
import jax
import jax.numpy as jnp
from jax import lax
from jax.sharding import PartitionSpec as P


def merged(value, axis, join):
    pieces = jax.tree.map(lambda part: lax.all_gather(part, axis), value)
    head = jax.tree.map(lambda part: part[0], pieces)
    tail = jax.tree.map(lambda part: part[1:], pieces)
    so_far, _ = lax.scan(lambda so_far, piece: (join(so_far, piece), None), head, tail)
    return so_far


def routing(owners, dp_count, rows_dev, capacity):
    target_owner = owners[:, 0]
    total_rows = target_owner.shape[0]
    columns = lax.broadcasted_iota(jnp.int32, (total_rows, dp_count), 1)
    onehot = (target_owner[:, None] == columns).astype(jnp.int32)
    blocks = onehot.reshape(dp_count, rows_dev, dp_count)
    before = jnp.sum((jnp.cumsum(blocks, axis=1) - blocks) * blocks, axis=2).reshape(total_rows)
    source = lax.broadcasted_iota(jnp.int32, (total_rows,), 0) // rows_dev
    slot_of = target_owner * (dp_count * capacity) + source * capacity + before
    return (slot_of, target_owner * capacity + before)


def inverse(slot_of, first_slot, slot_total):
    wanted = first_slot + lax.broadcasted_iota(jnp.int32, (slot_total, slot_of.shape[0]), 0)
    matches = (slot_of[None, :] == wanted).astype(jnp.int32)
    row_numbers = lax.broadcasted_iota(jnp.int32, matches.shape, 1)
    return (jnp.sum(matches * row_numbers, axis=1), jnp.sum(matches, axis=1))


def local_stats(logits, ref_values, target, first_col):
    row_peak = jnp.max(logits, axis=1)
    weights = jnp.exp(logits - row_peak[:, None])
    row_mass = jnp.sum(weights, axis=1)
    row_cross = jnp.sum(weights * (logits - ref_values), axis=1)
    ref_peak = jnp.max(ref_values, axis=1)
    ref_mass = jnp.sum(jnp.exp(ref_values - ref_peak[:, None]), axis=1)
    vocab_ids = first_col + lax.broadcasted_iota(jnp.int32, logits.shape, 1)
    picked = jnp.sum(jnp.where(vocab_ids == target[:, None], logits, 0.0), axis=1)
    return (row_peak, row_mass, row_cross, ref_peak, ref_mass, picked)


def combine(earlier, later):
    joint_peak = jnp.maximum(earlier[0], later[0])
    left_scale = jnp.exp(earlier[0] - joint_peak)
    right_scale = jnp.exp(later[0] - joint_peak)
    joint_ref = jnp.maximum(earlier[3], later[3])
    ref_mass = earlier[4] * jnp.exp(earlier[3] - joint_ref) + later[4] * jnp.exp(
        later[3] - joint_ref
    )
    return (
        joint_peak,
        earlier[1] * left_scale + later[1] * right_scale,
        earlier[2] * left_scale + later[2] * right_scale,
        joint_ref,
        ref_mass,
        earlier[5] + later[5],
    )


def finish(totals):
    row_peak, row_mass, row_cross, ref_peak, ref_mass, picked = totals
    log_norm = row_peak + jnp.log(row_mass)
    ref_norm = ref_peak + jnp.log(ref_mass)
    row_kl = row_cross / row_mass - log_norm + ref_norm
    return (log_norm, ref_norm, row_kl, picked - log_norm)


def logit_grad(
    logits,
    ref_values,
    target,
    first_col,
    log_norm,
    ref_norm,
    row_kl,
    lp_cotangent,
    kl_cotangent,
    filled,
):
    probs = jnp.exp(logits - log_norm[:, None])
    vocab_ids = first_col + lax.broadcasted_iota(jnp.int32, logits.shape, 1)
    is_target = (vocab_ids == target[:, None]).astype(jnp.float32)
    excess = logits - log_norm[:, None] - ref_values + ref_norm[:, None] - row_kl[:, None]
    result = lp_cotangent[:, None] * is_target + probs * (
        kl_cotangent[:, None] * excess - lp_cotangent[:, None]
    )
    return (result * filled[:, None]).astype(jnp.bfloat16)


def per_device(pol_hidden, pol_weight, ref_logits, targets, owners, grad_logprob, grad_kl):
    dp_count = lax.axis_size("dp")
    dp_index = lax.axis_index("dp")
    vocab_index = lax.axis_index("vocab")
    rows_dev = ref_logits.shape[0]
    vocab_dev = ref_logits.shape[1]
    all_slots = pol_hidden.shape[0]
    slot_count = all_slots // dp_count
    capacity = slot_count // dp_count
    first_col = vocab_index * vocab_dev
    slot_of, position = routing(owners, dp_count, rows_dev, capacity)
    own_positions = lax.dynamic_slice_in_dim(position, dp_index * rows_dev, rows_dev)
    position_grid = (
        lax.broadcasted_iota(jnp.int32, (slot_count, rows_dev), 0) == own_positions[None, :]
    )
    placing = position_grid.astype(jnp.bfloat16)
    outgoing = jnp.dot(placing, ref_logits, preferred_element_type=jnp.float32).astype(jnp.bfloat16)
    arrived = lax.all_to_all(
        outgoing.reshape(dp_count, capacity, vocab_dev),
        "dp",
        split_axis=0,
        concat_axis=0,
        tiled=True,
    )
    ref_values = arrived.reshape(slot_count, vocab_dev).astype(jnp.float32)
    ref_row, occupied = inverse(slot_of, dp_index * slot_count, slot_count)
    target = jnp.take(targets, ref_row)
    lp_cotangent = lax.dynamic_slice_in_dim(grad_logprob, dp_index * slot_count, slot_count)
    kl_cotangent = lax.dynamic_slice_in_dim(grad_kl, dp_index * slot_count, slot_count)
    logits = lax.psum_scatter(
        jnp.dot(pol_hidden, pol_weight, preferred_element_type=jnp.float32),
        "dp",
        scatter_dimension=0,
        tiled=True,
    )
    totals = merged(local_stats(logits, ref_values, target, first_col), "vocab", combine)
    log_norm, ref_norm, row_kl, row_logprob = finish(totals)
    filled = occupied.astype(jnp.float32)
    logit_grads = logit_grad(
        logits,
        ref_values,
        target,
        first_col,
        log_norm,
        ref_norm,
        row_kl,
        lp_cotangent,
        kl_cotangent,
        filled,
    )
    gathered = lax.all_gather(logit_grads, "dp", axis=0, tiled=True)
    feature_terms = lax.dot_general(
        gathered, pol_weight, (((1,), (1,)), ((), ())), preferred_element_type=jnp.float32
    )
    results = (row_logprob * filled, row_kl * filled, log_norm * filled)
    weight_grad = lax.dot_general(
        pol_hidden, gathered, (((0,), (0,)), ((), ())), preferred_element_type=jnp.float32
    ).astype(jnp.bfloat16)
    feature_grad = lax.psum_scatter(feature_terms, "vocab", scatter_dimension=0, tiled=True).astype(
        jnp.bfloat16
    )
    return (results[0], results[1], results[2], feature_grad, weight_grad)


def solution(mesh):
    in_specs = (P(None, "dp"), P("dp", "vocab"), P("dp", "vocab"), P(), P(), P(), P())
    out_specs = (P("dp"), P("dp"), P("dp"), P("vocab", "dp"), P("dp", "vocab"))
    return jax.shard_map(
        per_device, mesh=mesh, in_specs=in_specs, out_specs=out_specs, check_vma=False
    )
```

profile of v0, /device:TPU:1, one launch (start us, length us, event | category | flops | bytes accessed | tf_op | source)
XLA Modules:
  0.0 279.1 jit_solution(12646408732726949342)
XLA Ops:
  7.2 1.0 copy-done
  8.2 11.4 %fusion.34 = f32[512,8192]{1,0:T(8,128)} fusion(bf16[512,512]{1,0:T(8,128)(2,1)S(1)} %copy-done, bf16[512,8192]{1,0:T(8,128)(2,1)} %param.10), kind=kOutput, calls=%fused_computation.75 | convolution fusion | flops 4294967296 | bytes 25690112 | tf_op jit(solution)/shard_map/dot_general | solution.py:124
  19.7 0.5 broadcast.130
  20.3 0.7 broadcast_multiply_fusion
  21.2 0.5 fusion.33
  21.9 0.3 convolution_convert_fusion.1
  22.2 1.1 reshape.118
  23.3 7.6 %all-to-all-start = ((bf16[16,2,8192]{2,1,0:T(2,128)(2,1)}), bf16[16,2,8192]{2,1,0:T(2,128)(2,1)S(1)}, u32[]{:S(2)}, u32[]{:S(2)}) async-start(bf16[16,2,8192]{2,1,0:T(2,128)(2,1)} %reshape.118), calls=%async_computation.1 | async-start | bytes 1048576 | tf_op jit(solution)/shard_map/all_to_all | solution.py:111
  31.2 0.8 dynamic_slice.30
  31.9 0.8 dynamic_slice.29
  32.7 0.6 dynamic-slice
  33.9 0.7 gather_fusion
  34.7 9.0 %all-to-all-done = bf16[16,2,8192]{2,1,0:T(2,128)(2,1)S(1)} async-done(((bf16[16,2,8192]{2,1,0:T(2,128)(2,1)}), bf16[16,2,8192]{2,1,0:T(2,128)(2,1)S(1)}, u32[]{:S(2)}, u32[]{:S(2)}) %all-to-all-start) | async-done | bytes 524320 | tf_op jit(solution)/shard_map/all_to_all | solution.py:111
  43.7 0.5 reduce_max.28
  44.3 1.0 exponential_reduce_fusion
  45.4 15.3 %all-gather.4 = f32[8,1,32]{2,1,0:T(1,128)S(1)} all-gather(f32[1,1,32]{2,1,0:T(1,128)S(1)} %reshape.157), channel_id=1, replica_groups=mesh['dp'=16,'vocab'=8] {'vocab'}, dimensions={0}, use_global_device_ids=true | all-gather | bytes 1152 | tf_op jit(solution)/shard_map/all_gather | solution.py:8
  60.7 8.0 %all-gather.5 = f32[8,1,32]{2,1,0:T(1,128)S(1)} all-gather(f32[1,1,32]{2,1,0:T(1,128)S(1)} %reshape.159), channel_id=1, replica_groups=mesh['dp'=16,'vocab'=8] {'vocab'}, dimensions={0}, use_global_device_ids=true | all-gather | bytes 1152 | tf_op jit(solution)/shard_map/all_gather | solution.py:8
  68.9 69.9 %reduce-scatter.3.cloned.1.call-done = f32[32,8192]{1,0:T(8,128)} async-done(((f32[512,8192]{1,0:T(8,128)}), f32[32,8192]{1,0:T(8,128)}) %reduce-scatter.3.cloned.1.call-update) | async-done | bytes 1048592 | tf_op jit(solution)/shard_map/reduce_scatter | solution.py:123
  138.8 1.4 reduce_max.27
  140.2 0.2 dynamic-update-slice
  140.4 1.8 multiply_reduce_fusion
  142.9 12.9 %all-reduce.4 = (f32[256]{0:T(256)S(1)}, f32[256]{0:T(256)S(1)}, f32[256]{0:T(256)S(1)}, f32[256]{0:T(256)S(1)}) all-reduce(f32[256]{0:T(256)S(1)} %dynamic-update-slice, f32[256]{0:T(256)S(1)} %dynamic-update-slice.1, f32[256]{0:T(256)S(1)} %dynamic-update-slice.2, f32[256]{0:T(256)S(1)} %dynamic-update-slice.3), channel_id=2, replica_groups=mesh['dp'=16,'vocab'=8] {'vocab'}, use_global_device_ids=true, to_apply=%add | all-reduce | flops 1024 | bytes 8192
  156.4 0.7 while.20
  157.1 0.5 convert_multiply_fusion
  157.6 0.5 convert_multiply_fusion.1
  158.1 2.5 fusion.20
  160.9 69.9 %all-gather.8.cloned.1.call-done = bf16[512,8192]{1,0:T(8,128)(2,1)} async-done(((bf16[32,8192]{1,0:T(8,128)(2,1)}), bf16[512,8192]{1,0:T(8,128)(2,1)}) %all-gather.8.cloned.1.call-update) | async-done | bytes 8388624 | tf_op jit(solution)/shard_map/all_gather | solution.py:144
  230.8 11.3 %fusion.35 = f32[512,512]{1,0:T(8,128)} fusion(bf16[512,8192]{1,0:T(8,128)(2,1)} %all-gather.8.cloned.1.call-done, bf16[512,8192]{1,0:T(8,128)(2,1)} %param.10), kind=kOutput, calls=%fused_computation.76 | convolution fusion | flops 4294967296 | bytes 17825792 | tf_op jit(solution)/shard_map/dot_general | solution.py:145
  242.1 10.3 %fusion.15 = bf16[512,8192]{0,1:T(8,128)(2,1)} fusion(bf16[512,8192]{1,0:T(8,128)(2,1)} %all-gather.8.cloned.1.call-done, bf16[512,512]{1,0:T(8,128)(2,1)S(1)} %copy-done), kind=kOutput, calls=%fused_computation.25 | convolution fusion | flops 4299161600 | bytes 17301504 | tf_op jit(solution)/shard_map/dot_general | solution.py:149
  252.4 11.9 %copy.23 = bf16[512,8192]{1,0:T(8,128)(2,1)} copy(bf16[512,8192]{0,1:T(8,128)(2,1)} %fusion.15) | data formatting | bytes 16777216
  264.3 6.8 %reduce-scatter.5.cloned.1.call-done = f32[64,512]{1,0:T(8,128)} async-done(((f32[512,512]{1,0:T(8,128)}), f32[64,512]{1,0:T(8,128)}) %reduce-scatter.5.cloned.1.call-update) | async-done | bytes 131088 | tf_op jit(solution)/shard_map/reduce_scatter | solution.py:152
  271.1 1.5 convert_element_type.48
  (85 shorter events, 3.2 us)
Async XLA Ops:
  7.2 1.0 copy-start
  7.2 131.6 %reduce-scatter.3.cloned.1.call-start = ((), (), s32[]{:S(2)}) async-start(), calls=%async_computation.3 | async-start | bytes 17825792 | tf_op jit(solution)/shard_map/reduce_scatter | solution.py:123
  19.7 0.7 copy-start.3
  19.7 2.2 copy-start.2
  19.7 13.0 %copy-start.4 = (u32[128]{0:T(128)S(1)}, u32[128]{0:T(128)}, u32[]{:S(2)}) copy-start(u32[128]{0:T(128)} %constant.80) | copy-start | bytes 1540
  19.7 14.3 %copy-start.1 = (s32[256]{0:T(256)S(1)}, s32[256]{0:T(256)}, u32[]{:S(2)}) copy-start(s32[256]{0:T(256)} %param.12) | copy-start | bytes 3076
  23.3 20.4 %all-to-all-start = ((bf16[16,2,8192]{2,1,0:T(2,128)(2,1)}), bf16[16,2,8192]{2,1,0:T(2,128)(2,1)S(1)}, u32[]{:S(2)}, u32[]{:S(2)}) async-start(bf16[16,2,8192]{2,1,0:T(2,128)(2,1)} %reshape.118), calls=%async_computation.1 | async-start | bytes 1048576 | tf_op jit(solution)/shard_map/all_to_all | solution.py:111
  30.9 199.9 %all-gather.8.cloned.1.call-start = ((), (), s32[]{:S(2)}) async-start(), calls=%async_computation.4 | async-start | bytes 8912896 | tf_op jit(solution)/shard_map/all_gather | solution.py:144
  160.7 110.4 %reduce-scatter.5.cloned.1.call-start = ((), (), s32[]{:S(2)}) async-start(), calls=%async_computation.5 | async-start | bytes 1179648 | tf_op jit(solution)/shard_map/reduce_scatter | solution.py:152
Sparse Core Ops, SparseCore 0:
  19.8 118.9 reduce-scatter.2
  160.8 69.9 all-gather.7
  242.2 28.8 reduce-scatter.4
where the time goes:
time: 282 us; the launch traced here: 279 us
  waiting for transfers between devices  156 us (55%)
  blocking collectives  36.2 us (13%)
  matrix products  33.3 us (12%)
  local copies, waits for them, and re-layouts  19.8 us (7%)
  between operations  14.6 us (5%)
  other arithmetic  11.7 us (4%)
  starting transfers between devices  7.88 us (3%)
    reduce_scatter x1, waiting for transfers between devices, per_device(): lax.psum_scatter(jnp.dot(pol_hidden, pol_weight, preferred_element_type=j...  69.9 us
    all_gather x1, waiting for transfers between devices, per_device(): gathered = lax.all_gather(logit_grads, 'dp', axis=0, tiled=True)  69.9 us
    all_gather x2, blocking collectives, merged(): pieces = jax.tree.map(lambda part: lax.all_gather(part, axis), value)  23.3 us
    unnamed x25, local copies, waits for them, and re-layouts  15.2 us
    unnamed x1, blocking collectives  12.9 us
    dot_general x1, matrix products, per_device(): jnp.dot(pol_hidden, pol_weight, preferred_element_type=jnp.float32)  11.4 us
    dot_general x1, matrix products, per_device(): lax.dot_general(gathered, pol_weight, (((1,), (1,)), ((), ())), preferred...  11.3 us
    dot_general x1, matrix products, per_device(): lax.dot_general(pol_hidden, gathered, (((0,), (0,)), ((), ())), preferred...  10.3 us
  transfers between devices with their start and end apart: 4, of which 4 were waited for; matrix products, arithmetic and copies ran while one was open for 11% of the time, Pallas kernels for 0%

commit v1 on v0

--- a/solution.py
+++ b/solution.py
@@ -2,14 +2,6 @@
 import jax.numpy as jnp
 from jax import lax
 from jax.sharding import PartitionSpec as P
-
-
-def merged(value, axis, join):
-    pieces = jax.tree.map(lambda part: lax.all_gather(part, axis), value)
-    head = jax.tree.map(lambda part: part[0], pieces)
-    tail = jax.tree.map(lambda part: part[1:], pieces)
-    so_far, _ = lax.scan(lambda so_far, piece: (join(so_far, piece), None), head, tail)
-    return so_far
 
 
 def routing(owners, dp_count, rows_dev, capacity):
@@ -22,13 +14,6 @@
     source = lax.broadcasted_iota(jnp.int32, (total_rows,), 0) // rows_dev
     slot_of = target_owner * (dp_count * capacity) + source * capacity + before
     return (slot_of, target_owner * capacity + before)
-
-
-def inverse(slot_of, first_slot, slot_total):
-    wanted = first_slot + lax.broadcasted_iota(jnp.int32, (slot_total, slot_of.shape[0]), 0)
-    matches = (slot_of[None, :] == wanted).astype(jnp.int32)
-    row_numbers = lax.broadcasted_iota(jnp.int32, matches.shape, 1)
-    return (jnp.sum(matches * row_numbers, axis=1), jnp.sum(matches, axis=1))
 
 
 def local_stats(logits, ref_values, target, first_col):
@@ -101,34 +86,30 @@
     slot_count = all_slots // dp_count
     capacity = slot_count // dp_count
     first_col = vocab_index * vocab_dev
-    slot_of, position = routing(owners, dp_count, rows_dev, capacity)
-    own_positions = lax.dynamic_slice_in_dim(position, dp_index * rows_dev, rows_dev)
-    position_grid = (
-        lax.broadcasted_iota(jnp.int32, (slot_count, rows_dev), 0) == own_positions[None, :]
+    slot_of, _ = routing(owners, dp_count, rows_dev, capacity)
+    placing = slot_of[:, None] == lax.broadcasted_iota(
+        jnp.int32, (slot_of.shape[0], all_slots), 1
     )
-    placing = position_grid.astype(jnp.bfloat16)
-    outgoing = jnp.dot(placing, ref_logits, preferred_element_type=jnp.float32).astype(jnp.bfloat16)
-    arrived = lax.all_to_all(
-        outgoing.reshape(dp_count, capacity, vocab_dev),
-        "dp",
-        split_axis=0,
-        concat_axis=0,
-        tiled=True,
-    )
-    ref_values = arrived.reshape(slot_count, vocab_dev).astype(jnp.float32)
-    ref_row, occupied = inverse(slot_of, dp_index * slot_count, slot_count)
-    target = jnp.take(targets, ref_row)
-    lp_cotangent = lax.dynamic_slice_in_dim(grad_logprob, dp_index * slot_count, slot_count)
-    kl_cotangent = lax.dynamic_slice_in_dim(grad_kl, dp_index * slot_count, slot_count)
+    row_hidden = jnp.dot(
+        placing.astype(jnp.bfloat16), pol_hidden, preferred_element_type=jnp.float32
+    ).astype(jnp.bfloat16)
     logits = lax.psum_scatter(
-        jnp.dot(pol_hidden, pol_weight, preferred_element_type=jnp.float32),
+        jnp.dot(row_hidden, pol_weight, preferred_element_type=jnp.float32),
         "dp",
         scatter_dimension=0,
         tiled=True,
     )
-    totals = merged(local_stats(logits, ref_values, target, first_col), "vocab", combine)
+    own = lax.dynamic_slice_in_dim(placing, dp_index * rows_dev, rows_dev)
+    lp_cotangent = jnp.sum(jnp.where(own, grad_logprob[None, :], 0.0), axis=1)
+    kl_cotangent = jnp.sum(jnp.where(own, grad_kl[None, :], 0.0), axis=1)
+    target = lax.dynamic_slice_in_dim(targets, dp_index * rows_dev, rows_dev)
+    ref_values = ref_logits.astype(jnp.float32)
+    stats = jnp.stack(local_stats(logits, ref_values, target, first_col))
+    stats = lax.all_gather(stats, "vocab")
+    totals = tuple(stats[0])
+    for part in range(1, stats.shape[0]):
+        totals = combine(totals, tuple(stats[part]))
     log_norm, ref_norm, row_kl, row_logprob = finish(totals)
-    filled = occupied.astype(jnp.float32)
     logit_grads = logit_grad(
         logits,
         ref_values,
@@ -139,15 +120,24 @@
         row_kl,
         lp_cotangent,
         kl_cotangent,
-        filled,
+        jnp.ones_like(log_norm),
     )
     gathered = lax.all_gather(logit_grads, "dp", axis=0, tiled=True)
-    feature_terms = lax.dot_general(
+    rows = lax.all_gather(jnp.stack([row_logprob, row_kl, log_norm]), "dp", axis=1, tiled=True)
+    mine = lax.dynamic_slice_in_dim(placing, dp_index * slot_count, slot_count, axis=1)
+    results = jnp.sum(jnp.where(mine[None], rows[:, :, None], 0.0), axis=1)
+    feature_rows = lax.dot_general(
         gathered, pol_weight, (((1,), (1,)), ((), ())), preferred_element_type=jnp.float32
     )
-    results = (row_logprob * filled, row_kl * filled, log_norm * filled)
+    feature_terms = lax.dot_general(
+        placing.astype(jnp.float32),
+        feature_rows,
+        (((0,), (0,)), ((), ())),
+        precision=lax.Precision.HIGHEST,
+        preferred_element_type=jnp.float32,
+    )
     weight_grad = lax.dot_general(
-        pol_hidden, gathered, (((0,), (0,)), ((), ())), preferred_element_type=jnp.float32
+        row_hidden, gathered, (((0,), (0,)), ((), ())), preferred_element_type=jnp.float32
     ).astype(jnp.bfloat16)
     feature_grad = lax.psum_scatter(feature_terms, "vocab", scatter_dimension=0, tiled=True).astype(
         jnp.bfloat16

time: 282 us -> 225 us (0.80)
  waiting for transfers between devices: 156 us -> 137 us
  local copies, waits for them, and re-layouts: 19.8 us -> 2.54 us
  starting transfers between devices: 7.88 us -> 0.12 us
  matrix products: 33.3 us -> 26.2 us
    all_gather x1, waiting for transfers between devices: 69.9 us -> 49.8 us  [per_device(): gathered = lax.all_gather(logit_grads, 'dp', axis=0, tiled=True)]
    reduce_scatter x1, waiting for transfers between devices: 69.9 us -> 85.3 us  [per_device(): lax.psum_scatter(jnp.dot(row_hidden, pol_weight, preferred_element_type=j...]
    unnamed x25 -> x12, local copies, waits for them, and re-layouts: 15.2 us -> 1.41 us
    unnamed x1 -> x0, blocking collectives: 12.9 us -> none
    all_gather x2, blocking collectives: 23.3 us -> 33.5 us  [the longest x1 18.3 us: per_device(): lax.all_gather(jnp.stack([row_logprob, row_kl, log_norm]), 'dp', axis=1,...]
    all_to_all x1 -> x0, waiting for transfers between devices: 9.03 us -> none  [per_device(): lax.all_to_all(outgoing.reshape(dp_count, capacity, vocab_dev), 'dp', spl...]
    all_to_all x1 -> x0, starting transfers between devices: 7.58 us -> none  [per_device(): lax.all_to_all(outgoing.reshape(dp_count, capacity, vocab_dev), 'dp', spl...]
    reduce_scatter x1, waiting for transfers between devices: 6.77 us -> 1.66 us  [per_device(): lax.psum_scatter(feature_terms, 'vocab', scatter_dimension=0, tiled=True)]
  transfers between devices with their start and end apart: 4 -> 3, of which waited for: 4 -> 3; matrix products, arithmetic and copies ran while one was open for 11% -> 4% of each run, Pallas kernels for 0% -> 0%
where the time goes in v1:
time: 225 us; the launch traced here: 223 us
  waiting for transfers between devices  137 us (61%)
  blocking collectives  33.5 us (15%)
  matrix products  26.2 us (12%)
  between operations  13.9 us (6%)
  other arithmetic  9.53 us (4%)
  local copies, waits for them, and re-layouts  2.54 us (1%)
    reduce_scatter x1, waiting for transfers between devices, per_device(): lax.psum_scatter(jnp.dot(row_hidden, pol_weight, preferred_element_type=j...  85.3 us
    all_gather x1, waiting for transfers between devices, per_device(): gathered = lax.all_gather(logit_grads, 'dp', axis=0, tiled=True)  49.8 us
    all_gather x1, blocking collectives, per_device(): lax.all_gather(jnp.stack([row_logprob, row_kl, log_norm]), 'dp', axis=1,...  18.3 us
    all_gather x1, blocking collectives, per_device(): stats = lax.all_gather(stats, 'vocab')  15.2 us
    dot_general x1, matrix products, per_device(): jnp.dot(row_hidden, pol_weight, preferred_element_type=jnp.float32)  9.13 us
    dot_general x1, matrix products, per_device(): lax.dot_general(row_hidden, gathered, (((0,), (0,)), ((), ())), preferred...  7.99 us
    dot_general x1, matrix products, per_device(): lax.dot_general(gathered, pol_weight, (((1,), (1,)), ((), ())), preferred...  7.02 us
  transfers between devices with their start and end apart: 3, of which 3 were waited for; matrix products, arithmetic and copies ran while one was open for 4% of the time, Pallas kernels for 0%

profile of v1, /device:TPU:1, one launch (start us, length us, event | category | flops | bytes accessed | tf_op | source)
XLA Modules:
  0.0 222.6 jit_solution(1660312023774413634)
XLA Ops:
  7.2 0.5 broadcast.73
  7.7 1.3 reduce.4
  9.1 0.1 eq.33
  9.2 0.1 copy.20
  9.2 0.5 fusion.168
  9.8 0.1 reshape.1706
  9.9 0.7 fusion.21
  10.6 0.3 convolution_convert_fusion.1
  10.9 9.1 %fusion.169 = f32[256,8192]{1,0:T(8,128)} fusion(bf16[256,512]{1,0:T(8,128)(2,1)S(1)} %convolution_convert_fusion.1, bf16[512,8192]{1,0:T(8,128)(2,1)} %param.8), kind=kOutput, calls=%fused_computation.321 | convolution fusion | flops 2147483648 | bytes 17039360 | tf_op jit(solution)/shard_map/dot_general | solution.py:97
  20.1 0.6 copy-done.4
  20.7 0.1 dynamic_slice.10
  20.8 0.2 copy-done.1
  21.0 0.2 reduce_max.28
  21.2 0.1 iota_compare_fusion
  21.4 0.1 select_reduce_fusion.2
  21.5 85.3 %reduce-scatter.3.cloned.1.call-done = f32[16,8192]{1,0:T(8,128)} async-done(((f32[256,8192]{1,0:T(8,128)}), f32[16,8192]{1,0:T(8,128)}) %reduce-scatter.3.cloned.1.call-update) | async-done | bytes 524304 | tf_op jit(solution)/shard_map/reduce_scatter | solution.py:96
  106.9 1.2 reduce_max.27
  108.1 1.5 fusion.5
  109.6 15.2 %all-gather.1 = f32[8,6,16]{2,1,0:T(8,128)S(1)} all-gather(f32[1,6,16]{2,1,0:T(8,128)S(1)} %bitcast.958), channel_id=2, replica_groups=mesh['dp'=16,'vocab'=8] {'vocab'}, dimensions={0}, use_global_device_ids=true | all-gather | bytes 3456 | tf_op jit(solution)/shard_map/all_gather | solution.py:108
  124.8 2.0 fusion.3
  127.0 49.8 %all-gather.5.cloned.1.call-done = bf16[256,8192]{1,0:T(8,128)(2,1)} async-done(((bf16[16,8192]{1,0:T(8,128)(2,1)}), bf16[256,8192]{1,0:T(8,128)(2,1)}) %all-gather.5.cloned.1.call-update) | async-done | bytes 4194320 | tf_op jit(solution)/shard_map/all_gather | solution.py:125
  176.8 7.0 %fusion.170 = f32[256,512]{1,0:T(8,128)S(1)} fusion(bf16[256,8192]{1,0:T(8,128)(2,1)} %all-gather.5.cloned.1.call-done, bf16[512,8192]{1,0:T(8,128)(2,1)} %param.8), kind=kOutput, calls=%fused_computation.322 | convolution fusion | flops 2147483648 | bytes 13107200 | tf_op jit(solution)/shard_map/dot_general | solution.py:129
  183.8 1.7 fusion.14
  185.5 0.1 constant_dynamic-slice_fusion
  185.6 0.1 copy.22
  185.8 18.3 %all-gather.2 = f32[16,16,3]{1,2,0:T(4,128)S(1)} all-gather(f32[1,16,3]{1,2,0:T(4,128)S(1)} %maximum_bitcast_fusion), channel_id=1, replica_groups=mesh['dp'=16,'vocab'=8] {'dp'}, dimensions={0}, use_global_device_ids=true | all-gather | bytes 3264 | tf_op jit(solution)/shard_map/all_gather | solution.py:126
  204.1 0.1 reshape.1715
  204.2 0.1 select_reduce_fusion
  204.3 0.5 slice_bitcast_fusion
  204.8 8.0 %convolution_convert_fusion = bf16[512,8192]{1,0:T(8,128)(2,1)} fusion(bf16[256,512]{1,0:T(8,128)(2,1)S(1)} %convolution_convert_fusion.1, bf16[256,8192]{1,0:T(8,128)(2,1)} %all-gather.5.cloned.1.call-done), kind=kOutput, calls=%fused_computation | convolution fusion | flops 2151677952 | bytes 12845056 | tf_op jit(solution)/shard_map/dot_general | solution.py:139
  212.8 1.7 reduce-scatter.5.cloned.1.call-done
  214.5 1.5 convert_element_type.26
  (24 shorter events, 0.5 us)
Async XLA Ops:
  7.2 3.4 %copy-start = (bf16[512,512]{1,0:T(8,128)(2,1)S(1)}, bf16[512,512]{1,0:T(8,128)(2,1)}, u32[]{:S(2)}) copy-start(bf16[512,512]{1,0:T(8,128)(2,1)} %param.7) | copy-start | bytes 1572868
  7.2 99.7 %reduce-scatter.3.cloned.1.call-start = ((), (), s32[]{:S(2)}) async-start(), calls=%async_computation.2 | async-start | bytes 8912896 | tf_op jit(solution)/shard_map/reduce_scatter | solution.py:96
  20.1 0.7 copy-start.4
  20.1 1.0 copy-start.1
  20.1 1.3 copy-start.2
  20.1 1.3 copy-start.3
  20.1 156.7 %all-gather.5.cloned.1.call-start = ((), (), s32[]{:S(2)}) async-start(), calls=%async_computation.3 | async-start | bytes 4456448 | tf_op jit(solution)/shard_map/all_gather | solution.py:125
  126.9 87.6 %reduce-scatter.5.cloned.1.call-start = ((), (), s32[]{:S(2)}) async-start(), calls=%async_computation.4 | async-start | bytes 1179648 | tf_op jit(solution)/shard_map/reduce_scatter | solution.py:142
Sparse Core Ops, SparseCore 0:
  20.2 86.5 reduce-scatter.2
  127.0 49.6 all-gather.4
  185.6 28.8 reduce-scatter.4
